TPU v7x, 256 devices: a whole 4x4x8 slice. The times are simulated.
256 devices in a mesh: row: 16 (over z_lo, x, core), col: 16 (over z_hi, y).
Axes of the slice: x: 4, y: 4, z: 8 (z_hi: 4, z_lo: 2; z = z_hi * 2 + z_lo), core: 2. Of those that a mesh axis runs over, the one named last changes fastest.
Arguments:
- pair_input: bfloat16 [384, 384, 128], P('row', 'col'), may hold values from -6 to 6
- norm_mean: float32 [384, 384], P('row', 'col'), may hold values from -0.5 to 0.5
- norm_scale: float32 [384, 384], P('row', 'col'), may hold values from 0.5 to 2
- pair_mask: int32 [384, 384], P('row', 'col'), may hold values 0 or 1
- cotangent: bfloat16 [384, 384, 128], P('row', 'col'), may hold values from -6 to 6
- left_gate: bfloat16 [128, 128], replicated, may hold values from -0.5 to 0.5
- left_value: bfloat16 [128, 128], replicated, may hold values from -0.5 to 0.5
- right_gate: bfloat16 [128, 128], replicated, may hold values from -0.5 to 0.5
- right_value: bfloat16 [128, 128], replicated, may hold values from -0.5 to 0.5
- output_gate: bfloat16 [128, 128], replicated, may hold values from -0.5 to 0.5
- output_weight: bfloat16 [128, 128], replicated, may hold values from -0.5 to 0.5
Outputs:
- pair_grad: float32 [384, 384, 128], P('row', 'col')
Inputs may be any that keep to these rules, and one draw needn't show every extreme that they name: `pair_mask`: 1 marks a pair that takes part.
All inputs are finite; a program needn't handle non-finite values. No bound on the sum of `pair_mask` on one device may be relied on, other than what follows from the above.
Results may differ from a plain program's by a relative error of at most 0.0072.
Values may be sent and summed in bfloat16 or wider, within the bound.
No kernel may reach another device: no remote copies, remote signals or barrier semaphores. Data moves between devices by JAX's collectives and lax.ppermute only.
A program may use at most 128 MiB of HBM per device.

v0:
```python
import jax
import jax.numpy as jnp
from jax import lax
from jax.sharding import PartitionSpec as P

epsilon = 1e-05


def layer_back(grad, normed, scale):
    centre = jnp.mean(grad, axis=-1, keepdims=True)
    along = jnp.mean(grad * normed, axis=-1, keepdims=True)
    return scale * (grad - centre - normed * along)


def column_panel(right_edge):
    return lax.all_gather(right_edge, "row", axis=0, tiled=True)


def panel_right(right_edge):
    right_cols = column_panel(right_edge)
    return lax.all_to_all(right_cols, "col", split_axis=0, concat_axis=1, tiled=True)


def panel_grad_right(grad_mix, left_rows):
    partial_right = jnp.einsum(
        "ijh,ikh->jkh", grad_mix, left_rows, preferred_element_type=jnp.float32
    )
    moved_right = lax.all_to_all(partial_right, "col", split_axis=1, concat_axis=0, tiled=True)
    return lax.psum_scatter(moved_right, "row", scatter_dimension=0, tiled=True)


def per_device(
    pair_input,
    norm_mean,
    norm_scale,
    pair_mask,
    cotangent,
    left_gate,
    left_value,
    right_gate,
    right_value,
    output_gate,
    output_weight,
):
    rows_here, cols_here, width = pair_input.shape
    hidden = left_gate.shape[1]
    flat_rows = rows_here * cols_here
    normed = (pair_input.astype(jnp.float32) - norm_mean[:, :, None]) * norm_scale[:, :, None]
    normed_low = normed.astype(jnp.bfloat16)
    stacked = jnp.concatenate([left_gate, left_value, right_gate, right_value, output_gate], axis=1)
    projected = jnp.dot(
        normed_low.reshape(flat_rows, width), stacked, preferred_element_type=jnp.float32
    )
    keep = pair_mask.reshape(flat_rows, 1).astype(jnp.float32)
    left_sig = jax.nn.sigmoid(projected[:, :hidden])
    left_lin = projected[:, hidden : 2 * hidden]
    right_sig = jax.nn.sigmoid(projected[:, 2 * hidden : 3 * hidden])
    right_lin = projected[:, 3 * hidden : 4 * hidden]
    out_sig = jax.nn.sigmoid(projected[:, 4 * hidden :])
    left_edge = (
        (left_sig * left_lin * keep).astype(jnp.bfloat16).reshape(rows_here, cols_here, hidden)
    )
    right_edge = (
        (right_sig * right_lin * keep).astype(jnp.bfloat16).reshape(rows_here, cols_here, hidden)
    )
    left_rows = lax.all_gather(left_edge, "col", axis=1, tiled=True)
    right_mine = panel_right(right_edge)
    mixed = jnp.einsum("ikh,jkh->ijh", left_rows, right_mine, preferred_element_type=jnp.float32)
    centred = mixed - jnp.mean(mixed, axis=-1, keepdims=True)
    mix_scale = lax.rsqrt(jnp.mean(centred * centred, axis=-1, keepdims=True) + epsilon)
    mix_normed = centred * mix_scale
    out_lin = jnp.dot(
        mix_normed.astype(jnp.bfloat16).reshape(flat_rows, hidden),
        output_weight,
        preferred_element_type=jnp.float32,
    )
    upstream = cotangent.reshape(flat_rows, width).astype(jnp.float32)
    grad_y = (upstream * out_sig).astype(jnp.bfloat16)
    grad_gate = upstream * out_lin * out_sig * (1.0 - out_sig)
    grad_mixnorm = jnp.dot(grad_y, output_weight.T, preferred_element_type=jnp.float32).reshape(
        rows_here, cols_here, hidden
    )
    grad_mix = layer_back(grad_mixnorm, mix_normed, mix_scale).astype(jnp.bfloat16)
    partial_left = jnp.einsum(
        "ijh,jkh->ikh", grad_mix, right_mine, preferred_element_type=jnp.float32
    )
    grad_left = lax.psum_scatter(partial_left, "col", scatter_dimension=1, tiled=True)
    grad_right = panel_grad_right(grad_mix, left_rows)
    grad_left = grad_left.reshape(flat_rows, hidden) * keep
    grad_right = grad_right.reshape(flat_rows, hidden) * keep
    pre_grads = jnp.concatenate(
        [
            grad_left * left_lin * left_sig * (1.0 - left_sig),
            grad_left * left_sig,
            grad_right * right_lin * right_sig * (1.0 - right_sig),
            grad_right * right_sig,
            grad_gate,
        ],
        axis=1,
    ).astype(jnp.bfloat16)
    grad_normed = jnp.dot(pre_grads, stacked.T, preferred_element_type=jnp.float32).reshape(
        rows_here, cols_here, width
    )
    return layer_back(grad_normed, normed, norm_scale[:, :, None])


def solution(mesh):
    placed = (
        P("row", "col", None),
        P("row", "col"),
        P("row", "col"),
        P("row", "col"),
        P("row", "col", None),
        P(),
        P(),
        P(),
        P(),
        P(),
        P(),
    )
    return jax.shard_map(
        per_device, mesh=mesh, in_specs=placed, out_specs=P("row", "col", None), check_vma=False
    )
```

profile of v0, /device:TPU:8, one launch (start us, length us, event | category | flops | bytes accessed | tf_op | source)
XLA Modules:
  0.0 452.5 jit_solution(10674677785893327585)
XLA Ops:
  6.5 0.7 convert_element_type.41
  7.3 0.1 convert_element_type.42
  7.3 0.8 constant_dynamic-update-slice_fusion.4
  8.1 0.8 constant_dynamic-update-slice_fusion.3
  8.9 0.8 constant_dynamic-update-slice_fusion.2
  9.7 0.8 constant_dynamic-update-slice_fusion.1
  10.4 0.8 constant_dynamic-update-slice_fusion
  11.2 1.1 fusion.14
  12.3 0.3 fusion.23
  12.7 1.1 multiply_convert_fusion.5
  13.8 0.0 all-gather.5.cloned.1.call-start
  13.8 0.7 copy.80
  14.6 39.2 %all-gather.3.cloned.1.call-done = bf16[384,24,128]{2,1,0:T(8,128)(2,1)} async-done(((bf16[24,24,128]{2,1,0:T(8,128)(2,1)}), bf16[384,24,128]{2,1,0:T(8,128)(2,1)}) %all-gather.3.cloned.1.call-update) | async-done | bytes 2359312 | tf_op jit(solution)/shard_map/all_gather | solution.py:16
  53.8 9.6 %all-to-all-start = ((bf16[384,24,128]{2,1,0:T(8,128)(2,1)}), bf16[384,24,128]{2,1,0:T(8,128)(2,1)}, u32[]{:S(2)}, u32[]{:S(2)}) async-start(bf16[384,24,128]{2,1,0:T(8,128)(2,1)} %all-gather.3.cloned.1.call-done), calls=%async_computation | async-start | bytes 4718592 | tf_op jit(solution)/shard_map/all_to_all | solution.py:21
  63.5 0.3 fusion.21
  63.8 0.1 div.37
  63.9 82.3 %all-gather.5.cloned.1.call-done = bf16[24,384,128]{2,0,1:T(8,128)(2,1)} async-done(((bf16[24,24,128]{2,0,1:T(8,128)(2,1)}), bf16[24,384,128]{2,0,1:T(8,128)(2,1)}) %all-gather.5.cloned.1.call-update) | async-done | bytes 2359312 | tf_op jit(solution)/shard_map/all_gather | solution.py:66
  146.2 3.7 copy.82
  149.9 3.8 copy.79
  153.7 4.5 copy.90
  158.2 3.9 bitcast_reduce_fusion
  162.1 0.1 copy.85
  162.2 1.9 copy.83
  164.0 0.3 multiply_reduce_fusion.2
  164.3 0.1 copy.103
  164.4 0.1 copy.87
  164.5 0.3 multiply_reduce_fusion.1
  164.8 0.1 copy.104
  164.9 0.1 copy.89
  164.9 1.0 fusion.16
  166.0 0.4 copy.95
  166.4 4.8 %convolution_bitcast_fusion.1 = f32[24,384,128]{1,0,2:T(8,128)} fusion(bf16[24,384,128]{1,0,2:T(8,128)(2,1)} %copy.90, bf16[24,24,128]{0,1,2:T(8,128)(2,1)S(1)} %copy.95), kind=kOutput, calls=%fused_computation.1 | convolution fusion | flops 56623104 | bytes 7225344 | tf_op jit(solution)/shard_map/ijh,jkh->ikh/dot_general | solution.py:84
  171.3 6.1 %copy.92 = f32[24,384,128]{2,0,1:T(8,128)} copy(f32[24,384,128]{1,0,2:T(8,128)} %convolution_bitcast_fusion.1) | data formatting | bytes 9437184 | tf_op jit(solution)/shard_map/ijh,jkh->ikh/transpose | solution.py:84
  177.4 3.1 convolution_bitcast_fusion
  180.5 6.1 %copy.96 = f32[24,384,128]{2,0,1:T(8,128)} copy(f32[24,384,128]{1,0,2:T(8,128)} %convolution_bitcast_fusion) | data formatting | bytes 9437184 | tf_op jit(solution)/shard_map/ijh,ikh->jkh/transpose | solution.py:25
  186.6 146.0 %all_to_all.36 = f32[24,384,128]{2,0,1:T(8,128)S(1)} all-to-all(f32[24,384,128]{2,0,1:T(8,128)} %copy.96), channel_id=1, replica_groups=mesh['row'=16,'col'=16] {'col'}, dimensions={1} | all-to-all | bytes 9437184 | tf_op jit(solution)/shard_map/all_to_all | solution.py:28
  332.6 3.0 copy.98
  335.6 34.8 %reduce-scatter.3.cloned.1.call-done = f32[24,24,128]{2,0,1:T(8,128)} async-done(((f32[24,384,128]{2,0,1:T(8,128)}), f32[24,24,128]{2,0,1:T(8,128)}) %reduce-scatter.3.cloned.1.call-update) | async-done | bytes 294928 | tf_op jit(solution)/shard_map/reduce_scatter | solution.py:87
  370.4 1.0 copy.93
  371.4 70.7 %reduce-scatter.5.cloned.1.call-done = f32[24,24,128]{2,1,0:T(8,128)} async-done(((f32[384,24,128]{2,1,0:T(8,128)}), f32[24,24,128]{2,1,0:T(8,128)}) %reduce-scatter.5.cloned.1.call-update) | async-done | bytes 294928 | tf_op jit(solution)/shard_map/reduce_scatter | solution.py:29
  442.1 1.2 multiply_convert_fusion
  443.6 0.2 fusion.3
  443.8 0.5 fusion.22
  444.3 0.1 div.40
  444.4 0.3 multiply_reduce_fusion
  444.7 0.1 copy.99
  444.8 0.1 copy.100
  444.9 1.1 subtract_multiply_fusion
  (36 shorter events, 0.4 us)
Async XLA Ops:
  6.5 56.9 %copy-start = (bf16[128,128]{1,0:T(8,128)(2,1)S(1)}, bf16[128,128]{1,0:T(8,128)(2,1)}, u32[]{:S(2)}) copy-start(bf16[128,128]{1,0:T(8,128)(2,1)} %param.21) | copy-start | bytes 98308
  6.5 47.3 %all-gather.3.cloned.1.call-start = ((), (), s32[]{:S(2)}) async-start(), calls=%async_computation.4 | async-start | bytes 2506752 | tf_op jit(solution)/shard_map/all_gather | solution.py:16
  12.7 50.8 %copy-start.1 = (f32[576,640]{1,0:T(8,128)}, f32[576,640]{1,0:T(8,128)S(1)}, u32[]{:S(2)}) copy-start(f32[576,640]{1,0:T(8,128)S(1)} %fusion.23) | copy-start | bytes 4423684
  13.8 132.4 %all-gather.5.cloned.1.call-start = ((), (), s32[]{:S(2)}) async-start(), calls=%async_computation.5 | async-start | bytes 2506752 | tf_op jit(solution)/shard_map/all_gather | solution.py:66
  14.5 48.9 %copy-start.7 = (bf16[24,24,128]{2,1,0:T(8,128)(2,1)S(1)}, bf16[24,24,128]{2,1,0:T(8,128)(2,1)}, u32[]{:S(2)}) copy-start(bf16[24,24,128]{2,1,0:T(8,128)(2,1)} %param.15) | copy-start | bytes 442372
  53.8 96.1 %all-to-all-start = ((bf16[384,24,128]{2,1,0:T(8,128)(2,1)}), bf16[384,24,128]{2,1,0:T(8,128)(2,1)}, u32[]{:S(2)}, u32[]{:S(2)}) async-start(bf16[384,24,128]{2,1,0:T(8,128)(2,1)} %all-gather.3.cloned.1.call-done), calls=%async_computation | async-start | bytes 4718592 | tf_op jit(solution)/shard_map/all_to_all | solution.py:21
  63.4 307.0 %reduce-scatter.3.cloned.1.call-start = ((), (), s32[]{:S(2)}) async-start(), calls=%async_computation.6 | async-start | bytes 5013504 | tf_op jit(solution)/shard_map/reduce_scatter | solution.py:87
  177.3 264.8 %reduce-scatter.5.cloned.1.call-start = ((), (), s32[]{:S(2)}) async-start(), calls=%async_computation.7 | async-start | bytes 5013504 | tf_op jit(solution)/shard_map/reduce_scatter | solution.py:29
  335.6 106.5 %copy-start.2 = (f32[576,640]{1,0:T(8,128)S(1)}, f32[576,640]{1,0:T(8,128)}, u32[]{:S(2)}) copy-start(f32[576,640]{1,0:T(8,128)} %copy-done.1) | copy-start | bytes 4423684
  335.6 108.0 %copy-start.4 = (bf16[24,24,128]{2,1,0:T(8,128)(2,1)S(1)}, bf16[24,24,128]{2,1,0:T(8,128)(2,1)}, u32[]{:S(2)}) copy-start(bf16[24,24,128]{2,1,0:T(8,128)(2,1)} %get-tuple-element.13) | copy-start | bytes 442372
  335.6 108.0 %copy-start.8 = (bf16[24,24,128]{2,1,0:T(8,128)(2,1)S(1)}, bf16[24,24,128]{2,1,0:T(8,128)(2,1)}, u32[]{:S(2)}) copy-start(bf16[24,24,128]{2,1,0:T(8,128)(2,1)} %param.15) | copy-start | bytes 442372
  443.4 1.0 copy-start.3
  443.4 1.0 copy-start.5
  443.4 1.0 copy-start.6
Sparse Core Ops, SparseCore 0:
  13.9 39.8 all-gather.2
  56.2 89.9 all-gather.4
  177.5 192.8 reduce-scatter.2
  372.8 69.2 reduce-scatter.4
where the time goes:
time: 454 us; the launch traced here: 453 us
  waiting for transfers between devices  227 us (50%)
  blocking collectives  146 us (32%)
  local copies, waits for them, and re-layouts  35.9 us (8%)
  between operations  13.4 us (3%)
  matrix products  13.2 us (3%)
  starting transfers between devices  9.72 us (2%)
  other arithmetic  7.22 us (2%)
    all_to_all x1, blocking collectives, panel_grad_right(): lax.all_to_all(partial_right, 'col', split_axis=1, concat_axis=0, tiled=T...  146 us
    all_gather x1, waiting for transfers between devices, per_device(): left_rows = lax.all_gather(left_edge, 'col', axis=1, tiled=True)  82.3 us
    reduce_scatter x1, waiting for transfers between devices, panel_grad_right(): return lax.psum_scatter(moved_right, 'row', scatter_dimension=0, tiled=True)  70.7 us
    all_gather x1, waiting for transfers between devices, column_panel(): return lax.all_gather(right_edge, 'row', axis=0, tiled=True)  39.2 us
    reduce_scatter x1, waiting for transfers between devices, per_device(): lax.psum_scatter(partial_left, 'col', scatter_dimension=1, tiled=True)  34.8 us
    all_to_all x1, starting transfers between devices, panel_right(): lax.all_to_all(right_cols, 'col', split_axis=0, concat_axis=1, tiled=True)  9.59 us
  transfers between devices with their start and end apart: 5, of which 4 were waited for; matrix products, arithmetic and copies ran while one was open for 4% of the time, Pallas kernels for 0%

commit v1 on v0

--- a/solution.py
+++ b/solution.py
@@ -13,7 +13,10 @@
 
 
 def column_panel(right_edge):
-    return lax.all_gather(right_edge, "row", axis=0, tiled=True)
+    _move_domain = lambda named_axis, z: jnp.concatenate(
+        lax.all_to_all(jnp.stack(lax.psum(1, named_axis) * [z]), named_axis, 0, 0), axis=0
+    )
+    return _move_domain("row", right_edge)
 
 
 def panel_right(right_edge):

time: 454 us -> 432 us (0.952)
  waiting for transfers between devices: 227 us -> 198 us
  starting transfers between devices: 9.72 us -> 16.7 us
    all_gather x1 -> x0, waiting for transfers between devices: 39.2 us -> none  [column_panel(): return lax.all_gather(right_edge, 'row', axis=0, tiled=True)]
    all_to_all x0 -> x1, waiting for transfers between devices: none -> 35.6 us  [column_panel(): lax.all_to_all(jnp.stack(lax.psum(1, named_axis) * [z]), named_axis, 0, 0)]
    all_gather x1, waiting for transfers between devices: 82.3 us -> 48.1 us  [per_device(): left_rows = lax.all_gather(left_edge, 'col', axis=1, tiled=True)]
    all_to_all x1, waiting for transfers between devices: 0.01 us -> 19.8 us  [panel_right(): lax.all_to_all(right_cols, 'col', split_axis=0, concat_axis=1, tiled=True)]
    reduce_scatter x1, waiting for transfers between devices: 34.8 us -> 23.5 us  [per_device(): lax.psum_scatter(partial_left, 'col', scatter_dimension=1, tiled=True)]
    all_to_all x0 -> x1, starting transfers between devices: none -> 5.8 us  [column_panel(): lax.all_to_all(jnp.stack(lax.psum(1, named_axis) * [z]), named_axis, 0, 0)]
  transfers between devices with their start and end apart: 5 -> 5, of which waited for: 4 -> 5; matrix products, arithmetic and copies ran while one was open for 4% -> 4% of each run, Pallas kernels for 0% -> 0%
where the time goes in v1:
time: 432 us; the launch traced here: 431 us
  waiting for transfers between devices  198 us (46%)
  blocking collectives  146 us (34%)
  local copies, waits for them, and re-layouts  37.7 us (9%)
  starting transfers between devices  16.7 us (4%)
  between operations  13.4 us (3%)
  matrix products  13.2 us (3%)
  other arithmetic  6.35 us (1%)
    all_to_all x1, blocking collectives, panel_grad_right(): lax.all_to_all(partial_right, 'col', split_axis=1, concat_axis=0, tiled=T...  146 us
    reduce_scatter x1, waiting for transfers between devices, panel_grad_right(): return lax.psum_scatter(moved_right, 'row', scatter_dimension=0, tiled=True)  70.8 us
    all_gather x1, waiting for transfers between devices, per_device(): left_rows = lax.all_gather(left_edge, 'col', axis=1, tiled=True)  48.1 us
    all_to_all x1, waiting for transfers between devices, column_panel(): lax.all_to_all(jnp.stack(lax.psum(1, named_axis) * [z]), named_axis, 0, 0)  35.6 us
    reduce_scatter x1, waiting for transfers between devices, per_device(): lax.psum_scatter(partial_left, 'col', scatter_dimension=1, tiled=True)  23.5 us
    all_to_all x1, waiting for transfers between devices, panel_right(): lax.all_to_all(right_cols, 'col', split_axis=0, concat_axis=1, tiled=True)  19.8 us
    all_to_all x1, starting transfers between devices, panel_right(): lax.all_to_all(right_cols, 'col', split_axis=0, concat_axis=1, tiled=True)  10.8 us
  transfers between devices with their start and end apart: 5, of which 5 were waited for; matrix products, arithmetic and copies ran while one was open for 4% of the time, Pallas kernels for 0%

profile of v1, /device:TPU:8, one launch (start us, length us, event | category | flops | bytes accessed | tf_op | source)
XLA Modules:
  0.0 431.3 jit_solution(156978451513321441)
XLA Ops:
  6.5 0.7 convert_element_type.41
  7.3 0.1 convert_element_type.42
  7.3 0.8 constant_dynamic-update-slice_fusion.4
  8.1 0.8 constant_dynamic-update-slice_fusion.3
  8.9 0.8 constant_dynamic-update-slice_fusion.2
  9.6 0.8 constant_dynamic-update-slice_fusion.1
  10.4 0.8 constant_dynamic-update-slice_fusion
  11.2 1.1 fusion.14
  12.3 0.3 fusion.23
  12.7 0.2 multiply_convert_fusion.5
  12.9 1.9 stack.3
  14.7 5.8 %all-to-all-start = ((bf16[16,24,24,128]{3,2,1,0:T(8,128)(2,1)}), bf16[16,24,24,128]{3,2,1,0:T(8,128)(2,1)}, u32[]{:S(2)}, u32[]{:S(2)}) async-start(bf16[16,24,24,128]{3,2,1,0:T(8,128)(2,1)} %stack.3), calls=%async_computation | async-start | bytes 4718592 | tf_op jit(solution)/shard_map/all_to_all | solution.py:17
  20.6 0.7 copy.80
  21.3 35.6 %all-to-all-done = bf16[16,24,24,128]{3,2,1,0:T(8,128)(2,1)} async-done(((bf16[16,24,24,128]{3,2,1,0:T(8,128)(2,1)}), bf16[16,24,24,128]{3,2,1,0:T(8,128)(2,1)}, u32[]{:S(2)}, u32[]{:S(2)}) %all-to-all-start) | async-done | bytes 2359328 | tf_op jit(solution)/shard_map/all_to_all | solution.py:17
  56.9 10.8 %all-to-all-start.1 = ((bf16[384,24,128]{2,1,0:T(8,128)(2,1)}), bf16[384,24,128]{2,1,0:T(8,128)(2,1)}, u32[]{:S(2)}, u32[]{:S(2)}) async-start(bf16[384,24,128]{2,1,0:T(8,128)(2,1)} %bitcast.2), calls=%async_computation.1 | async-start | bytes 4718592 | tf_op jit(solution)/shard_map/all_to_all | solution.py:24
  67.8 0.3 fusion.21
  68.1 0.1 div.37
  68.2 48.1 %all-gather.2.cloned.1.call-done = bf16[24,384,128]{2,0,1:T(8,128)(2,1)} async-done(((bf16[24,24,128]{2,0,1:T(8,128)(2,1)}), bf16[24,384,128]{2,0,1:T(8,128)(2,1)}) %all-gather.2.cloned.1.call-update) | async-done | bytes 2359312 | tf_op jit(solution)/shard_map/all_gather | solution.py:69
  116.3 3.7 copy.82
  120.0 19.8 %all-to-all-done.1 = bf16[384,24,128]{2,1,0:T(8,128)(2,1)} async-done(((bf16[384,24,128]{2,1,0:T(8,128)(2,1)}), bf16[384,24,128]{2,1,0:T(8,128)(2,1)}, u32[]{:S(2)}, u32[]{:S(2)}) %all-to-all-start.1) | async-done | bytes 2359328 | tf_op jit(solution)/shard_map/all_to_all | solution.py:24
  139.8 3.8 copy.79
  143.6 4.5 %copy.90 = bf16[24,384,128]{1,0,2:T(8,128)(2,1)} copy(bf16[24,384,128]{2,1,0:T(8,128)(2,1)} %bitcast.62) | data formatting | bytes 4718592 | tf_op jit(solution)/shard_map/all_to_all | solution.py:24
  148.1 3.9 bitcast_reduce_fusion
  152.0 0.1 copy.85
  152.1 1.9 copy.83
  154.0 0.3 multiply_reduce_fusion.2
  154.3 0.1 copy.87
  154.4 0.3 multiply_reduce_fusion.1
  154.7 0.1 copy.104
  154.8 0.1 copy.89
  154.9 1.0 fusion.16
  155.9 0.4 copy.95
  156.3 4.9 %convolution_bitcast_fusion.1 = f32[24,384,128]{1,0,2:T(8,128)} fusion(bf16[24,384,128]{1,0,2:T(8,128)(2,1)} %copy.90, bf16[24,24,128]{0,1,2:T(8,128)(2,1)S(1)} %copy.95), kind=kOutput, calls=%fused_computation.1 | convolution fusion | flops 56623104 | bytes 7225344 | tf_op jit(solution)/shard_map/ijh,jkh->ikh/dot_general | solution.py:87
  161.2 6.0 %copy.92 = f32[24,384,128]{2,0,1:T(8,128)} copy(f32[24,384,128]{1,0,2:T(8,128)} %convolution_bitcast_fusion.1) | data formatting | bytes 9437184 | tf_op jit(solution)/shard_map/ijh,jkh->ikh/transpose | solution.py:87
  167.3 3.1 convolution_bitcast_fusion
  170.4 6.1 %copy.96 = f32[24,384,128]{2,0,1:T(8,128)} copy(f32[24,384,128]{1,0,2:T(8,128)} %convolution_bitcast_fusion) | data formatting | bytes 9437184 | tf_op jit(solution)/shard_map/ijh,ikh->jkh/transpose | solution.py:28
  176.5 146.0 %all_to_all.41 = f32[24,384,128]{2,0,1:T(8,128)S(1)} all-to-all(f32[24,384,128]{2,0,1:T(8,128)} %copy.96), channel_id=1, replica_groups=mesh['row'=16,'col'=16] {'col'}, dimensions={1} | all-to-all | bytes 9437184 | tf_op jit(solution)/shard_map/all_to_all | solution.py:31
  322.6 3.0 copy.98
  325.6 23.5 %reduce-scatter.3.cloned.1.call-done = f32[24,24,128]{2,0,1:T(8,128)} async-done(((f32[24,384,128]{2,0,1:T(8,128)}), f32[24,24,128]{2,0,1:T(8,128)}) %reduce-scatter.3.cloned.1.call-update) | async-done | bytes 294928 | tf_op jit(solution)/shard_map/reduce_scatter | solution.py:90
  349.1 1.0 copy.93
  350.1 70.8 %reduce-scatter.5.cloned.1.call-done = f32[24,24,128]{2,1,0:T(8,128)} async-done(((f32[384,24,128]{2,1,0:T(8,128)}), f32[24,24,128]{2,1,0:T(8,128)}) %reduce-scatter.5.cloned.1.call-update) | async-done | bytes 294928 | tf_op jit(solution)/shard_map/reduce_scatter | solution.py:32
  420.9 1.2 multiply_convert_fusion
  422.4 0.2 fusion.3
  422.6 0.5 fusion.22
  423.1 0.1 div.40
  423.2 0.3 multiply_reduce_fusion
  423.6 0.1 copy.100
  423.7 1.1 subtract_multiply_fusion
  (36 shorter events, 0.5 us)
Async XLA Ops:
  6.5 61.2 %copy-start = (bf16[128,128]{1,0:T(8,128)(2,1)S(1)}, bf16[128,128]{1,0:T(8,128)(2,1)}, u32[]{:S(2)}) copy-start(bf16[128,128]{1,0:T(8,128)(2,1)} %param.21) | copy-start | bytes 98308
  12.7 55.1 %copy-start.1 = (f32[576,640]{1,0:T(8,128)}, f32[576,640]{1,0:T(8,128)S(1)}, u32[]{:S(2)}) copy-start(f32[576,640]{1,0:T(8,128)S(1)} %fusion.23) | copy-start | bytes 4423684
  14.7 42.2 %all-to-all-start = ((bf16[16,24,24,128]{3,2,1,0:T(8,128)(2,1)}), bf16[16,24,24,128]{3,2,1,0:T(8,128)(2,1)}, u32[]{:S(2)}, u32[]{:S(2)}) async-start(bf16[16,24,24,128]{3,2,1,0:T(8,128)(2,1)} %stack.3), calls=%async_computation | async-start | bytes 4718592 | tf_op jit(solution)/shard_map/all_to_all | solution.py:17
  20.5 95.8 %all-gather.2.cloned.1.call-start = ((), (), s32[]{:S(2)}) async-start(), calls=%async_computation.5 | async-start | bytes 2506752 | tf_op jit(solution)/shard_map/all_gather | solution.py:69
  56.9 10.9 %copy-start.7 = (bf16[24,24,128]{2,1,0:T(8,128)(2,1)S(1)}, bf16[24,24,128]{2,1,0:T(8,128)(2,1)}, u32[]{:S(2)}) copy-start(bf16[24,24,128]{2,1,0:T(8,128)(2,1)} %param.15) | copy-start | bytes 442372
  56.9 82.9 %all-to-all-start.1 = ((bf16[384,24,128]{2,1,0:T(8,128)(2,1)}), bf16[384,24,128]{2,1,0:T(8,128)(2,1)}, u32[]{:S(2)}, u32[]{:S(2)}) async-start(bf16[384,24,128]{2,1,0:T(8,128)(2,1)} %bitcast.2), calls=%async_computation.1 | async-start | bytes 4718592 | tf_op jit(solution)/shard_map/all_to_all | solution.py:24
  67.7 281.4 %reduce-scatter.3.cloned.1.call-start = ((), (), s32[]{:S(2)}) async-start(), calls=%async_computation.6 | async-start | bytes 5013504 | tf_op jit(solution)/shard_map/reduce_scatter | solution.py:90
  167.3 253.7 %reduce-scatter.5.cloned.1.call-start = ((), (), s32[]{:S(2)}) async-start(), calls=%async_computation.7 | async-start | bytes 5013504 | tf_op jit(solution)/shard_map/reduce_scatter | solution.py:32
  325.6 95.4 %copy-start.2 = (f32[576,640]{1,0:T(8,128)S(1)}, f32[576,640]{1,0:T(8,128)}, u32[]{:S(2)}) copy-start(f32[576,640]{1,0:T(8,128)} %copy-done.1) | copy-start | bytes 4423684
  325.6 96.8 %copy-start.4 = (bf16[24,24,128]{2,1,0:T(8,128)(2,1)S(1)}, bf16[24,24,128]{2,1,0:T(8,128)(2,1)}, u32[]{:S(2)}) copy-start(bf16[24,24,128]{2,1,0:T(8,128)(2,1)} %get-tuple-element.13) | copy-start | bytes 442372
  325.6 96.8 %copy-start.8 = (bf16[24,24,128]{2,1,0:T(8,128)(2,1)S(1)}, bf16[24,24,128]{2,1,0:T(8,128)(2,1)}, u32[]{:S(2)}) copy-start(bf16[24,24,128]{2,1,0:T(8,128)(2,1)} %param.15) | copy-start | bytes 442372
  422.2 1.0 copy-start.3
  422.2 1.0 copy-start.5
  422.2 1.0 copy-start.6
Sparse Core Ops, SparseCore 0:
  23.8 92.4 all-gather.1
  167.4 181.6 reduce-scatter.2
  351.6 69.2 reduce-scatter.4
